TPU v7x, 512 devices: a whole 4x8x8 slice. The times are simulated.
512 devices in a mesh: seq: 16 (over x, z_hi), head: 32 (over y, z_lo, core).
Axes of the slice: x: 4, y: 8, z: 8 (z_hi: 4, z_lo: 2; z = z_hi * 2 + z_lo), core: 2. Of those that a mesh axis runs over, the one named last changes fastest.
Arguments:
- queries: bfloat16 [4096, 4096], P('seq', 'head'), may hold values from -8 to 8
- block_keys: bfloat16 [4096, 512], P('seq'), may hold values from -8 to 8
- block_values: bfloat16 [4096, 512], P('seq'), may hold values from -12 to 12
- cache_keys: bfloat16 [4, 16384, 128], P(None, 'seq'), may hold values from -6 to 6
- cache_values: bfloat16 [4, 16384, 128], P(None, 'seq'), may hold values from -12 to 12
- lengths: int32 [8], replicated, may hold values from 1 to 4096, 16384 in all
- row_request: int32 [4096], P('seq'), may hold values from 0 to 7, never falling along the last dimension, each value on 1 to 4089 neighbouring positions
- positions: int32 [4096], P('seq'), may hold values from 0 to 1023
- out_weight: bfloat16 [4096, 4096], P('head'), may hold values from -0.375 to 0.375
Outputs:
- attended: bfloat16 [4096, 4096], P('seq', 'head')
Inputs may be any that keep to these rules, and one draw needn't show every extreme that they name: `row_request`: rows of one request stand together, requests in increasing order; one request has 4089 rows and every other request exactly one. Every request has at least one committed token; the lengths sum to 16384.
All inputs are finite; a program needn't handle non-finite values.
Results may differ from a plain program's by a relative error of at most 0.014.
Values may be sent and summed in bfloat16 or wider, within the bound.
A program may use at most 64 MiB of HBM per device.

v0:
```python
import math

import jax
import jax.numpy as jnp
from jax import lax
from jax.sharding import PartitionSpec as P

HEADS = 32
KVH = 4
HD = 128


rope_base = 10000.0
neg_floor = -1e30


def rotate_half_dims(vectors, rotary_pos):
    half_dim = vectors.shape[-1] // 2
    quarter = half_dim // 2
    freqs = jnp.exp(-math.log(rope_base) * jnp.arange(quarter, dtype=jnp.float32) / quarter)
    angles = rotary_pos[:, None] * freqs[None, :]
    cosine = jnp.cos(angles)[:, None, :]
    sine = jnp.sin(angles)[:, None, :]
    first = vectors[..., :quarter]
    second = vectors[..., quarter:half_dim]
    return jnp.concatenate(
        [first * cosine - second * sine, second * cosine + first * sine, vectors[..., half_dim:]],
        axis=-1,
    )


def absorb_block(stats, q_rows, row_lower, row_upper, request, key_rows, value_rows, key_tags):
    maxima, totals, summed = stats
    row_count = q_rows.shape[0]
    heads_q = q_rows.reshape(row_count, -1, HD)
    scores = jnp.einsum("rhd,kd->rhk", heads_q, key_rows, preferred_element_type=jnp.float32) * (
        1.0 / math.sqrt(HD)
    )
    visible = (key_tags[None, :] >= row_lower[:, None]) & (
        key_tags[None, :] < row_upper[:, None]
    ) | (key_tags[None, :] == -(request[:, None] + 1))
    visible = visible[:, None, :]
    running_top = jnp.maximum(maxima, jnp.max(jnp.where(visible, scores, neg_floor), axis=-1))
    correction = jnp.exp(maxima - running_top)
    weights = jnp.where(visible, jnp.exp(scores - running_top[..., None]), 0.0)
    totals = totals * correction + jnp.sum(weights, axis=-1)
    summed = summed * correction[..., None] + jnp.einsum(
        "rhk,kd->rhd", weights.astype(jnp.bfloat16), value_rows, preferred_element_type=jnp.float32
    )
    return (running_top, totals, summed)


def absorb(stats, q_rows, row_lower, row_upper, request, key_rows, value_rows, key_tags):
    key_count = key_rows.shape[0]
    block_len = key_count
    while block_len > 2048 and block_len % 2 == 0:
        block_len = block_len // 2
    pieces = key_count // block_len

    def scan_step(carry, inputs):
        return (
            absorb_block(
                carry, q_rows, row_lower, row_upper, request, inputs[0], inputs[1], inputs[2]
            ),
            None,
        )

    result, unused = lax.scan(
        scan_step,
        stats,
        (
            key_rows.reshape(pieces, block_len, HD),
            value_rows.reshape(pieces, block_len, HD),
            key_tags.reshape(pieces, block_len),
        ),
    )
    return result


def fresh_stats(row_count, head_count):
    return (
        jnp.full((row_count, head_count), neg_floor, jnp.float32),
        jnp.zeros((row_count, head_count), jnp.float32),
        jnp.zeros((row_count, head_count, HD), jnp.float32),
    )


def shards(
    queries,
    block_keys,
    block_values,
    cache_keys,
    cache_values,
    lengths,
    row_request,
    positions,
    out_weight,
):
    row_count = queries.shape[0]
    head_count = queries.shape[1] // HD
    group_size = HEADS // KVH
    kv_group = lax.axis_index("head") * head_count // group_size
    starts = jnp.cumsum(lengths) - lengths
    chooser = row_request[:, None] == jnp.arange(lengths.shape[0], dtype=jnp.int32)[None, :]
    row_len = jnp.sum(jnp.where(chooser, lengths[None, :], 0), axis=1)
    row_lower = jnp.sum(jnp.where(chooser, starts[None, :], 0), axis=1)
    row_upper = row_lower + row_len
    rotary_pos = (row_len + positions).astype(jnp.float32)
    q_rot = (
        rotate_half_dims(queries.reshape(row_count, head_count, HD).astype(jnp.float32), rotary_pos)
        .astype(jnp.bfloat16)
        .reshape(row_count, head_count * HD)
    )
    own_keys = lax.dynamic_slice_in_dim(block_keys, kv_group * HD, HD, 1)
    own_keys = (
        rotate_half_dims(own_keys.reshape(row_count, 1, HD).astype(jnp.float32), rotary_pos)
        .astype(jnp.bfloat16)
        .reshape(row_count, HD)
    )
    own_values = lax.dynamic_slice_in_dim(block_values, kv_group * HD, HD, 1)
    shard_keys = lax.dynamic_index_in_dim(cache_keys, kv_group, 0, keepdims=False)
    shard_values = lax.dynamic_index_in_dim(cache_values, kv_group, 0, keepdims=False)
    ctx_rows = shard_keys.shape[0]
    offset = lax.axis_index("seq") * ctx_rows
    key_rows = jnp.concatenate([shard_keys, own_keys], axis=0)
    value_rows = jnp.concatenate([shard_values, own_values], axis=0)
    key_tags = jnp.concatenate([offset + jnp.arange(ctx_rows, dtype=jnp.int32), -(row_request + 1)])
    maxima, totals, summed = absorb(
        fresh_stats(row_count, head_count),
        q_rot,
        row_lower,
        row_upper,
        row_request,
        lax.all_gather(key_rows, "seq", axis=0, tiled=True),
        lax.all_gather(value_rows, "seq", axis=0, tiled=True),
        lax.all_gather(key_tags, "seq", axis=0, tiled=True),
    )
    heads_out = (
        (summed / totals[..., None]).reshape(row_count, head_count * HD).astype(jnp.bfloat16)
    )
    partial_out = jnp.dot(heads_out, out_weight, preferred_element_type=jnp.float32)
    return lax.psum_scatter(partial_out, "head", scatter_dimension=1, tiled=True).astype(
        jnp.bfloat16
    )


def solution(mesh):
    placed = (
        P("seq", "head"),
        P("seq", None),
        P("seq", None),
        P(None, "seq", None),
        P(None, "seq", None),
        P(),
        P("seq"),
        P("seq"),
        P("head", None),
    )
    return jax.shard_map(
        shards, mesh=mesh, in_specs=placed, out_specs=P("seq", "head"), check_vma=False
    )
```

profile of v0, /device:TPU:1, one launch (start us, length us, event | category | flops | bytes accessed | tf_op | source)
XLA Modules:
  0.0 399.5 jit_solution(15880356774242667532)
XLA Ops:
  6.6 0.9 dynamic-slice_bitcast_fusion.2
  7.7 0.8 reduce-window.9
  9.2 0.9 copy.25
  10.3 0.8 select_reduce_fusion.1
  12.1 1.0 dynamic-slice_bitcast_fusion.1
  13.1 0.8 pad_maximum_fusion
  13.9 0.9 constant_dynamic-slice_fusion
  14.8 1.0 dynamic-slice_bitcast_fusion
  15.7 0.8 pad_maximum_fusion.1
  17.0 45.0 %all-gather = s32[16,1,1280]{2,1,0:T(1,128)S(1)} all-gather(s32[1,1,1280]{2,1,0:T(1,128)S(1)} %reshape.227), channel_id=1, replica_groups=mesh['seq'=16,'head'=32] {'seq'}, dimensions={0}, use_global_device_ids=true | all-gather | bytes 87040 | tf_op jit(solution)/shard_map/all_gather | solution.py:136
  62.2 47.0 %all-gather.4.cloned.1.call-done = bf16[20480,128]{1,0:T(8,128)(2,1)} async-done(((bf16[1280,128]{1,0:T(8,128)(2,1)}), bf16[20480,128]{1,0:T(8,128)(2,1)}) %all-gather.4.cloned.1.call-update) | async-done | bytes 5242896 | tf_op jit(solution)/shard_map/all_gather | solution.py:134
  109.1 95.1 %all-gather.6.cloned.1.call-done = bf16[20480,128]{1,0:T(8,128)(2,1)} async-done(((bf16[1280,128]{1,0:T(8,128)(2,1)}), bf16[20480,128]{1,0:T(8,128)(2,1)}) %all-gather.6.cloned.1.call-update) | async-done | bytes 5242896 | tf_op jit(solution)/shard_map/all_gather | solution.py:135
  204.2 58.9 %while.15 = (s32[]{:T(128)}, f32[256,1]{0,1:T(1,128)S(1)}, f32[256,1]{0,1:T(1,128)S(1)}, f32[256,1,128]{2,0,1:T(8,128)S(1)}, s32[16,1280]{1,0:T(8,128)S(1)}, /*i...) while((s32[]{:T(128)}, f32[256,1]{0,1:T(1,128)S(1)}, ...), condition=%wide.region_6.7_spmd.clone, body=%wide.region_3.6_spmd.clone.sunk | while | flops 175736576 | bytes 4969613 | solution.py:68
  204.2 1.5 select_reduce_fusion.4
  206.2 1.6 fusion.50
  207.9 1.5 select_reduce_fusion.4
  209.9 1.6 fusion.50
  211.6 1.5 select_reduce_fusion.4
  213.6 1.6 fusion.50
  215.3 1.5 select_reduce_fusion.4
  217.3 1.6 fusion.50
  219.0 1.5 select_reduce_fusion.4
  220.9 1.6 fusion.50
  222.6 1.5 select_reduce_fusion.4
  224.6 1.6 fusion.50
  226.3 1.5 select_reduce_fusion.4
  228.3 1.6 fusion.50
  230.0 1.5 select_reduce_fusion.4
  232.0 1.6 fusion.50
  233.7 1.5 select_reduce_fusion.4
  235.7 1.6 fusion.50
  237.4 1.5 select_reduce_fusion.4
  239.4 1.6 fusion.50
  241.1 1.5 select_reduce_fusion.4
  243.0 1.6 fusion.50
  244.8 1.5 select_reduce_fusion.4
  246.7 1.6 fusion.50
  248.4 1.5 select_reduce_fusion.4
  250.4 1.6 fusion.50
  252.1 1.5 select_reduce_fusion.4
  254.1 1.6 fusion.50
  255.8 1.5 select_reduce_fusion.4
  257.8 1.6 fusion.50
  259.5 1.5 select_reduce_fusion.4
  261.5 1.6 fusion.50
  263.1 2.7 fusion.18
  265.8 125.6 %reduce-scatter.2.cloned.1.call-done = f32[256,128]{1,0:T(8,128)} async-done(((f32[256,4096]{1,0:T(8,128)}), f32[256,128]{1,0:T(8,128)}) %reduce-scatter.2.cloned.1.call-update) | async-done | bytes 131088 | tf_op jit(solution)/shard_map/reduce_scatter | solution.py:142
  391.4 1.5 convert_element_type.48
  (131 shorter events, 10.2 us)
Async XLA Ops:
  6.5 256.6 %copy-start = (bf16[128,4096]{1,0:T(8,128)(2,1)S(1)}, bf16[128,4096]{1,0:T(8,128)(2,1)}, u32[]{:S(2)}) copy-start(bf16[128,4096]{1,0:T(8,128)(2,1)} %param.19) | copy-start | bytes 3145732
  6.5 102.6 %all-gather.4.cloned.1.call-start = ((), (), s32[]{:S(2)}) async-start(), calls=%async_computation.1 | async-start | bytes 5570560 | tf_op jit(solution)/shard_map/all_gather | solution.py:134
  13.1 3.5 copy-start.1
  13.9 3.1 copy-start.2
  13.9 190.3 %all-gather.6.cloned.1.call-start = ((), (), s32[]{:S(2)}) async-start(), calls=%async_computation.2 | async-start | bytes 5570560 | tf_op jit(solution)/shard_map/all_gather | solution.py:135
  16.5 374.9 %reduce-scatter.2.cloned.1.call-start = ((), (), s32[]{:S(2)}) async-start(), calls=%async_computation.3 | async-start | bytes 4325376 | tf_op jit(solution)/shard_map/reduce_scatter | solution.py:142
Sparse Core Ops, SparseCore 0:
  14.0 95.0 all-gather.3
  112.2 91.9 all-gather.5
  266.0 125.4 reduce-scatter.1
where the time goes:
time: 403 us; the launch traced here: 400 us
  waiting for transfers between devices  268 us (67%)
  matrix products  53.1 us (13%)
  blocking collectives  45 us (11%)
  other arithmetic  13.6 us (3%)
  between operations  13.3 us (3%)
  local copies, waits for them, and re-layouts  5.87 us (1%)
    reduce_scatter x1, waiting for transfers between devices, shards(): lax.psum_scatter(partial_out, 'head', scatter_dimension=1, tiled=True)  126 us
    all_gather x1, waiting for transfers between devices, shards(): lax.all_gather(value_rows, 'seq', axis=0, tiled=True)  95.1 us
    all_gather x1, waiting for transfers between devices, shards(): lax.all_gather(key_rows, 'seq', axis=0, tiled=True)  47 us
    all_gather x1, blocking collectives, shards(): lax.all_gather(key_tags, 'seq', axis=0, tiled=True)  45 us
    dot_general x16, matrix products, absorb_block(): jnp.einsum('rhk,kd->rhd', weights.astype(jnp.bfloat16), value_rows, prefe...  26.3 us
    dot_general x16, matrix products, absorb_block(): jnp.einsum('rhd,kd->rhk', heads_q, key_rows, preferred_element_type=jnp.f...  24.2 us
  transfers between devices with their start and end apart: 3, of which 3 were waited for; matrix products, arithmetic and copies ran while one was open for 1% of the time, Pallas kernels for 0%

commit v1 on v0

v1 whole, which is shorter than its diff:
```python
import math

import jax
import jax.numpy as jnp
from jax import lax
from jax.experimental import pallas as pl
from jax.experimental.pallas import tpu as pltpu
from jax.sharding import PartitionSpec as P

HD = 128
REQS = 8
BIG = 4089
MASKED = -1e30
SCALE = math.log2(math.e) / math.sqrt(HD)
LN2 = math.log(2.0)

bf16 = jnp.bfloat16
f32 = jnp.float32
i32 = jnp.int32
MESH = pl.DeviceIdType.MESH


def kernel(
    len_s, req_s, req_v, pos_v, q_h, bk_h, bv_h, ck_h, cv_h, w_h,
    out_ref,
    qraw, kraw, cosb, sinb, qbuf, qhot, cand, gkv, bias, cks, cvs, qs, sp, spr,
    ob, tb, lb, osend, ssend, orecv, srecv, hbuf, wbuf, psend, precv,
    loc, sq, rq, sc, rc, sz, rz, sg, rg, ss, rs, sw, rw, so, ro, sl, rl, sh, rh, sf, rf,
):
    seq = lax.axis_index("seq")
    head = lax.axis_index("head")
    x, zh = seq // 4, seq % 4
    g, m = head // 8, head % 8
    chip, core = m // 2, m % 2

    def xpeer(k):
        return (((x + k) % 4) * 4 + zh, head)

    def zpeer(k):
        return (x * 4 + (zh + k) % 4, head)

    def gpeer(k, other):
        c = (1 - core) if other else core
        return (seq, g * 8 + ((chip + k) % 4) * 2 + c)

    def fpeer(k):
        return (seq, ((g + k) % 4) * 8 + m)

    def remote(src, dst, ssem, rsem, peer):
        return pltpu.make_async_remote_copy(
            src_ref=src, dst_ref=dst, send_sem=ssem, recv_sem=rsem,
            device_id=peer, device_id_type=MESH,
        )

    piece = pl.multiple_of(32 * m, 32)
    gcol = pl.multiple_of(g * 128, 128)
    mycand = pl.multiple_of(256 * x + 32 * m, 32)
    c_q = pltpu.make_async_copy(q_h, qraw, loc.at[0])
    c_k = pltpu.make_async_copy(bk_h.at[pl.ds(piece, 32), pl.ds(gcol, 128)], kraw, loc.at[1])
    c_v = pltpu.make_async_copy(
        bv_h.at[pl.ds(piece, 32), pl.ds(gcol, 128)], gkv.at[0, 1, 0, 0, 0], loc.at[2]
    )
    c_ck = pltpu.make_async_copy(ck_h.at[g, pl.ds(mycand, 32)], cand.at[0, 0], loc.at[3])
    c_cv = pltpu.make_async_copy(cv_h.at[g, pl.ds(mycand, 32)], cand.at[1, 0], loc.at[4])
    c_sk = pltpu.make_async_copy(ck_h.at[g], cks, loc.at[5])
    c_sv = pltpu.make_async_copy(cv_h.at[g], cvs, loc.at[6])
    for c in (c_q, c_k, c_v, c_ck, c_cv, c_sk, c_sv):
        c.start()

    barrier = pltpu.get_barrier_semaphore()
    peers = [xpeer(k) for k in (1, 2, 3)] + [zpeer(k) for k in (1, 2, 3)]
    peers += [gpeer(k, o) for k in range(4) for o in (False, True) if k or o]
    peers += [fpeer(k) for k in (1, 3)]
    for peer in peers:
        pl.semaphore_signal(barrier, inc=1, device_id=peer, device_id_type=MESH)

    row_len = jnp.zeros((2, 128), i32)
    for r in range(REQS):
        row_len = jnp.where(req_v[...] == r, len_s[r], row_len)
    rotary = (row_len + pos_v[...]).astype(f32)
    spread = jnp.concatenate(
        [jnp.transpose(jnp.broadcast_to(rotary[h : h + 1, :], (128, 128))) for h in (0, 1)], axis=0
    )
    lane8 = lax.broadcasted_iota(i32, (8, 128), 1)
    freqs = jnp.zeros((8, 128), f32)
    for k in range(HD // 4):
        freqs = jnp.where((lane8 < 64) & (lane8 % 32 == k), 10000.0 ** (-k / (HD // 4)), freqs)
    angles = spread * freqs[0:1, :]
    lane256 = lax.broadcasted_iota(i32, (256, 128), 1)
    cosb[...] = jnp.cos(angles)
    sine = jnp.sin(angles)
    sinb[...] = jnp.where(lane256 < 32, -sine, sine)

    def rotate(v, cosine, signed, lane):
        partner = jnp.where(lane < 32, pltpu.roll(v, 96, 1), pltpu.roll(v, 32, 1))
        return v * cosine + partner * signed

    pl.semaphore_wait(barrier, len(peers))

    order = (2, 1, 3)
    cand_c, q_c, blk_c = [], [], []
    for k in order:
        start = pl.multiple_of(256 * ((x + k) % 4) + 32 * m, 32)
        cand_c.append(remote(ck_h.at[g, pl.ds(start, 32)], cand.at[0, k], sc.at[0, k], rc.at[0, k], xpeer(k)))
        cand_c.append(remote(cv_h.at[g, pl.ds(start, 32)], cand.at[1, k], sc.at[1, k], rc.at[1, k], xpeer(k)))
        blk_c.append(
            remote(gkv.at[0, :, 0, 0, 0], gkv.at[0, :, 0, 0, k], sz.at[0, k], rz.at[0, k], zpeer(k))
        )
        q_c.append(remote(qbuf.at[0], qbuf.at[k], sq.at[k], rq.at[k], xpeer(k)))
    for c in cand_c:
        c.start()

    c_k.wait()
    gkv[0, 0, 0, 0, 0] = rotate(
        kraw[...].astype(f32), cosb[pl.ds(piece, 32), :], sinb[pl.ds(piece, 32), :],
        lax.broadcasted_iota(i32, (32, 128), 1),
    ).astype(bf16)
    c_v.wait()
    for c in blk_c:
        c.start()
    c_q.wait()
    qbuf[0] = rotate(qraw[...].astype(f32), cosb[...], sinb[...], lane256).astype(bf16)
    for c in q_c:
        c.start()

    def blocks_start(kc, ko):
        mm = ((chip + kc) % 4) * 2 + ((1 - core) if ko else core)
        for j in range(4):
            col = pl.multiple_of((((g + j) % 4) * 8 + mm) * 128, 128)
            src = w_h.at[:, pl.ds(col, 128)]
            dst = wbuf.at[kc, ko, :, j * 128 : (j + 1) * 128]
            if kc == 0 and ko == 0:
                pltpu.make_async_copy(src, dst, loc.at[7]).start()
            else:
                remote(src, dst, sw.at[kc, ko], rw.at[kc, ko], gpeer(kc, ko == 1)).start()

    blocks_start(0, 0)
    blocks_start(0, 1)

    big = req_s[128]
    first = jnp.int32(0)
    span = jnp.int32(0)
    run = jnp.int32(0)
    low8 = jnp.zeros((8, 128), i32)
    high8 = jnp.zeros((8, 128), i32)
    for r in range(REQS):
        size = len_s[r]
        hit = big == r
        first = jnp.where(hit, run, first)
        span = jnp.where(hit, size, span)
        low8 = jnp.where(lane8 == r, run, low8)
        run = run + size
        high8 = jnp.where(lane8 == r, run, high8)
    high8 = jnp.where(lane8 == big, low8, high8)

    def request_of(row):
        return jnp.where(row < big, row, jnp.where(row < big + BIG, big, row - (BIG - 1)))

    for c in cand_c:
        c.wait_recv()
    c_ck.wait()
    c_cv.wait()
    row32 = lax.broadcasted_iota(i32, (32, 128), 0)
    for t in (0, 1):
        chosen = jnp.zeros((32, 128), f32)
        for k in range(4):
            token = 4096 * ((x + 4 - k) % 4) + 1024 * zh + 256 * x + 32 * m + row32
            ok = (token >= first) & (token < first + span)
            chosen = jnp.where(ok, cand[t, k].astype(f32), chosen)
        gkv[1, t, 0, 0, 0] = chosen.astype(bf16)
    zc_c = [
        remote(gkv.at[1, :, 0, 0, 0], gkv.at[1, :, 0, 0, k], sz.at[1, k], rz.at[1, k], zpeer(k))
        for k in order
    ]
    for c in zc_c:
        c.start()

    def spread_start(kind):
        cs = [
            remote(gkv.at[kind, :, 0, 0], gkv.at[kind, :, k, 0], sg.at[kind, k, 0], rg.at[kind, k, 0], gpeer(k, False))
            for k in (1, 2, 3)
        ]
        cs.append(
            remote(gkv.at[kind, :, 0, 0], gkv.at[kind, :, 0, 1], sg.at[kind, 0, 1], rg.at[kind, 0, 1], gpeer(0, True))
        )
        for c in cs:
            c.start()
        return cs

    def relay(kind, cs):
        fs = []
        for k in (1, 2, 3):
            cs[k - 1].wait_recv()
            f = remote(
                gkv.at[kind, :, k, 0], gkv.at[kind, :, k, 1], sg.at[kind, k, 1], rg.at[kind, k, 1], gpeer(0, True)
            )
            f.start()
            fs.append(f)
        return fs

    def relay_wait(cs, fs):
        cs[3].wait_recv()
        for f in fs:
            f.wait_recv()

    for c in blk_c:
        c.wait_recv()
    blk_g = spread_start(0)

    for c in q_c:
        c.wait_recv()
    at0, at3 = x, (x + 1) % 4
    qs[0, 0:16, :] = qbuf[at0, 0:16, :]
    qs[0, 16:32, :] = qbuf[at3, 240:256, :]
    qs_c = [remote(qs.at[0], qs.at[k], ss.at[0, k], rs.at[0, k], zpeer(k)) for k in order]
    for c in qs_c:
        c.start()

    for c in zc_c:
        c.wait_recv()
    cache_g = spread_start(1)

    key = lax.broadcasted_iota(i32, (1024, 128), 0)
    lane1024 = lax.broadcasted_iota(i32, (1024, 128), 1)
    key_chip = (chip + 4 - (key >> 8)) & 3
    key_core = (core + (key >> 7)) & 1
    key_z = (zh + 4 - (key >> 5)) & 3
    inner = 32 * (key_chip * 2 + key_core) + (key & 31)
    block_req = request_of(1024 * x + 256 * key_z + inner)
    bias[0] = jnp.where(lane1024 == block_req, 0.0, MASKED).astype(bf16)
    slot = 1024 * key_z + 256 * x + inner
    inside = ((slot - first) & 4095) < span
    bias[1] = jnp.where(inside & (lane1024 == big), 0.0, MASKED).astype(bf16)
    row256 = lax.broadcasted_iota(i32, (256, 128), 0)
    for k in range(4):
        row = 256 * (4 * ((x + 4 - k) % 4) + zh) + row256
        qhot[k] = jnp.where(lane256 == request_of(row), 1.0, 0.0).astype(bf16)

    def attend(kind, k, v_t):
        k_aug = jnp.concatenate([gkv[kind, 0].reshape(1024, 128), bias[kind]], axis=1)
        q_aug = jnp.concatenate([qbuf[k], qhot[k]], axis=1)
        s = lax.dot_general(k_aug, q_aug, (((1,), (1,)), ((), ())), preferred_element_type=f32)
        top = jnp.max(s, axis=0, keepdims=True) * SCALE
        p = jnp.exp2(s * SCALE - top)
        total = jnp.sum(p, axis=0, keepdims=True)
        o = jnp.dot(v_t, p.astype(bf16), preferred_element_type=f32)
        return o, top, total

    def merge(o1, t1, l1, o2, t2, l2):
        top = jnp.maximum(t1, t2)
        w1, w2 = jnp.exp2(t1 - top), jnp.exp2(t2 - top)
        return o1 * w1 + o2 * w2, top, l1 * w1 + l2 * w2

    for c in qs_c:
        c.wait_recv()
    c_sk.wait()
    c_sv.wait()
    row128 = lax.broadcasted_iota(i32, (128, 128), 0)
    lane128 = lax.broadcasted_iota(i32, (128, 128), 1)
    from_z = (zh + 4 - (row128 >> 5)) & 3
    late = (row128 >> 4) & 1
    qs_row = 256 * from_z + (row128 & 15) + late * (3072 + 240)
    qs_hot = jnp.where(lane128 == request_of(qs_row), 1.0, 0.0).astype(bf16)
    token = 1024 * seq + key
    seen = (token >= low8[0:1, :]) & (token < high8[0:1, :])
    own_bias = jnp.where(seen, 0.0, MASKED).astype(bf16)
    s = lax.dot_general(
        jnp.concatenate([qs[...].reshape(128, 128), qs_hot], axis=1),
        jnp.concatenate([cks[...], own_bias], axis=1),
        (((1,), (1,)), ((), ())), preferred_element_type=f32,
    )
    top = jnp.max(s, axis=1, keepdims=True) * SCALE
    p = jnp.exp2(s * SCALE - top)
    total = jnp.sum(p, axis=1, keepdims=True)
    o = jnp.dot(p.astype(bf16), cvs[...], preferred_element_type=f32) / total
    lse = jnp.broadcast_to(top + jnp.log(total) * (1.0 / LN2), (128, 128))
    sp[:, 0] = o.reshape(4, 32, 128)
    sp[:, 1] = lse.reshape(4, 32, 128)
    sp_c = [
        remote(sp.at[k], spr.at[k], ss.at[1, k], rs.at[1, k], (x * 4 + (zh + 4 - k) % 4, head)) for k in order
    ]
    for c in sp_c:
        c.start()

    blk_f = relay(0, blk_g)
    relay_wait(blk_g, blk_f)

    vt0 = jnp.transpose(gkv[0, 1].reshape(1024, 128))

    def block_step(k, carry):
        o, t, l = attend(0, k, vt0)
        ob[k] = o
        tb[k] = jnp.broadcast_to(t, (8, 256))
        lb[k] = jnp.broadcast_to(l, (8, 256))
        return carry

    lax.fori_loop(0, 4, block_step, 0)

    cache_f = relay(1, cache_g)
    for kc in (2, 1, 3):
        blocks_start(kc, 0)
        blocks_start(kc, 1)

    for c in sp_c:
        c.wait_recv()
    o, t, l = sp[0, 0], sp[0, 1], jnp.ones((32, 128), f32)
    for k in (1, 2, 3):
        o, t, l = merge(o, t, l, spr[k, 0], spr[k, 1], 1.0)
    pad = jnp.zeros((96, 128), f32)
    o, t, l = [jnp.transpose(jnp.concatenate([a, pad], axis=0)) for a in (o, t, l)]
    for at, half, shift, own in ((at0, 0, 0, lane128 < 16), (at3, 1, 96, lane128 >= 112)):
        cols = slice(128 * half, 128 * half + 128)
        o2, t2, l2 = [pltpu.roll(a, shift, 1) if shift else a for a in (o, t, l)]
        t2 = jnp.where(own, t2, MASKED)[0:8, :]
        l2 = l2[0:8, :]
        t1, l1 = tb[at, :, cols], lb[at, :, cols]
        top = jnp.maximum(t1, t2)
        w1, w2 = jnp.exp2(t1 - top), jnp.exp2(t2 - top)
        tb[at, :, cols] = top
        lb[at, :, cols] = l1 * w1 + l2 * w2
        ob[at, :, cols] = ob[at, :, cols] * w1[0:1, :] + jnp.where(own, o2, 0.0) * w2[0:1, :]

    relay_wait(cache_g, cache_f)
    vt1 = jnp.transpose(gkv[1, 1].reshape(1024, 128))
    o_c = []
    for k in order + (0,):
        o, t, l = attend(1, k, vt1)
        o, t, l = merge(ob[k], tb[k, 0:1, :], lb[k, 0:1, :], o, t, l)
        osend[k] = (o * (1.0 / l)).astype(bf16)
        ssend[k] = jnp.broadcast_to(t + jnp.log(l) * (1.0 / LN2), (8, 256))
        if k:
            back = (((x + 4 - k) % 4) * 4 + zh, head)
            o_c.append(remote(osend.at[k], orecv.at[k], so.at[k], ro.at[k], back))
            o_c.append(remote(ssend.at[k], srecv.at[k], sl.at[k], rl.at[k], back))
            o_c[-2].start()
            o_c[-1].start()
    for c in o_c:
        c.wait_recv()

    lses = [ssend[0, 0:1, :]] + [srecv[k, 0:1, :] for k in (1, 2, 3)]
    top = jnp.maximum(jnp.maximum(lses[0], lses[1]), jnp.maximum(lses[2], lses[3]))
    weights = [jnp.exp2(l - top) for l in lses]
    total = 1.0 / (weights[0] + weights[1] + weights[2] + weights[3])
    h_c = []
    for half in (0, 1):
        cols = slice(128 * half, 128 * half + 128)
        heads = osend[0, :, cols].astype(f32) * (weights[0] * total)[:, cols]
        for k in (1, 2, 3):
            heads = heads + orecv[k, :, cols].astype(f32) * (weights[k] * total)[:, cols]
        hbuf[half, 0, 0] = jnp.transpose(heads).astype(bf16)
        cs = [
            remote(
                hbuf.at[half, 0, 0], hbuf.at[half, k, 0], sh.at[half, k, 0], rh.at[half, k, 0], gpeer(k, False)
            )
            for k in order
        ]
        cs.append(
            remote(hbuf.at[half, 0, 0], hbuf.at[half, 0, 1], sh.at[half, 0, 1], rh.at[half, 0, 1], gpeer(0, True))
        )
        for c in cs:
            c.start()
        h_c.append(cs)
    h_f = []
    for half in (0, 1):
        fs = []
        for n, k in enumerate(order):
            h_c[half][n].wait_recv()
            f = remote(
                hbuf.at[half, k, 0], hbuf.at[half, k, 1], sh.at[half, k, 1], rh.at[half, k, 1], gpeer(0, True)
            )
            f.start()
            fs.append(f)
        h_f.append(fs)

    w_wait = []
    for kc in range(4):
        for ko in (0, 1):
            if kc or ko:
                w_wait.append(
                    remote(w_h.at[:, 0:512], wbuf.at[kc, ko], sw.at[kc, ko], rw.at[kc, ko], gpeer(kc, ko == 1))
                )
    for c in w_wait:
        c.wait_recv()
    pltpu.make_async_copy(w_h.at[:, 0:512], wbuf.at[0, 0], loc.at[7]).wait()

    own, mids, finals = [], [], []
    for half in (0, 1):
        h_c[half][3].wait_recv()
        for f in h_f[half]:
            f.wait_recv()
        lhs = jnp.concatenate([hbuf[half, kc, ko] for kc in range(4) for ko in (0, 1)], axis=1)
        acc = jnp.dot(lhs, wbuf[...].reshape(1024, 512), preferred_element_type=f32)
        fwd, bwd = (1, 3) if half == 0 else (3, 1)
        psend[half, 2] = acc[:, 256:384].astype(bf16)
        psend[half, bwd] = acc[:, bwd * 128 : bwd * 128 + 128].astype(bf16)
        mid = remote(psend.at[half, 2], precv.at[half, 2], sf.at[half, 2], rf.at[half, 2], fpeer(fwd))
        near = remote(psend.at[half, bwd], precv.at[half, bwd], sf.at[half, bwd], rf.at[half, bwd], fpeer(bwd))
        mid.start()
        near.start()
        mids.append(mid)
        finals.append(near)
        own.append((acc[:, 0:128], acc[:, fwd * 128 : fwd * 128 + 128]))
    for half in (0, 1):
        fwd = 1 if half == 0 else 3
        mids[half].wait_recv()
        psend[half, fwd] = (own[half][1] + precv[half, 2].astype(f32)).astype(bf16)
        far = remote(psend.at[half, fwd], precv.at[half, fwd], sf.at[half, fwd], rf.at[half, fwd], fpeer(fwd))
        far.start()
        finals.append(far)
    for half in (0, 1):
        finals[half].wait_recv()
        finals[2 + half].wait_recv()
        total = own[half][0] + precv[half, 1].astype(f32) + precv[half, 3].astype(f32)
        out_ref[128 * half : 128 * half + 128, :] = total.astype(bf16)

    sent = cand_c + q_c + blk_c + zc_c + blk_g + blk_f + cache_g + cache_f + qs_c + sp_c
    sent += w_wait + o_c + h_c[0] + h_c[1] + h_f[0] + h_f[1] + mids + finals
    for c in sent:
        c.wait_send()


def shards(queries, block_keys, block_values, cache_keys, cache_values, lengths, row_request, positions, out_weight):
    dma = pltpu.SemaphoreType.DMA
    vmem = pltpu.VMEM
    return pl.pallas_call(
        kernel,
        out_shape=jax.ShapeDtypeStruct((256, HD), bf16),
        in_specs=[pl.BlockSpec(memory_space=pltpu.SMEM)] * 2
        + [pl.BlockSpec(memory_space=pltpu.VMEM)] * 2
        + [pl.BlockSpec(memory_space=pl.ANY)] * 6,
        out_specs=pl.BlockSpec(memory_space=pltpu.VMEM),
        scratch_shapes=[
            vmem((256, 128), bf16),
            vmem((32, 128), bf16),
            vmem((256, 128), f32),
            vmem((256, 128), f32),
            vmem((4, 256, 128), bf16),
            vmem((4, 256, 128), bf16),
            vmem((2, 4, 32, 128), bf16),
            vmem((2, 2, 4, 2, 4, 32, 128), bf16),
            vmem((2, 1024, 128), bf16),
            vmem((1024, 128), bf16),
            vmem((1024, 128), bf16),
            vmem((4, 32, 128), bf16),
            vmem((4, 2, 32, 128), f32),
            vmem((4, 2, 32, 128), f32),
            vmem((4, 128, 256), f32),
            vmem((4, 8, 256), f32),
            vmem((4, 8, 256), f32),
            vmem((4, 128, 256), bf16),
            vmem((4, 8, 256), f32),
            vmem((4, 128, 256), bf16),
            vmem((4, 8, 256), f32),
            vmem((2, 4, 2, 128, 128), bf16),
            vmem((4, 2, 128, 512), bf16),
            vmem((2, 4, 128, 128), bf16),
            vmem((2, 4, 128, 128), bf16),
            dma((8,)),
            dma((4,)), dma((4,)),
            dma((2, 4)), dma((2, 4)),
            dma((2, 4)), dma((2, 4)),
            dma((2, 4, 2)), dma((2, 4, 2)),
            dma((2, 4)), dma((2, 4)),
            dma((4, 2)), dma((4, 2)),
            dma((4,)), dma((4,)),
            dma((4,)), dma((4,)),
            dma((2, 4, 2)), dma((2, 4, 2)),
            dma((2, 4)), dma((2, 4)),
        ],
        compiler_params=pltpu.CompilerParams(
            collective_id=0, has_side_effects=True, vmem_limit_bytes=63 * 1024 * 1024
        ),
    )(
        lengths, row_request, row_request.reshape(2, 128), positions.reshape(2, 128),
        queries, block_keys, block_values, cache_keys, cache_values, out_weight,
    )


def solution(mesh):
    placed = (
        P("seq", "head"),
        P("seq", None),
        P("seq", None),
        P(None, "seq", None),
        P(None, "seq", None),
        P(),
        P("seq"),
        P("seq"),
        P("head", None),
    )
    return jax.shard_map(
        shards, mesh=mesh, in_specs=placed, out_specs=P("seq", "head"), check_vma=False
    )
```

time: 403 us -> 61.4 us (0.15)
  waiting for transfers between devices: 268 us -> 0 us
  Pallas kernels: 0 us -> 59.5 us
  matrix products: 53.1 us -> 0 us
  blocking collectives: 45 us -> 0 us
  other arithmetic: 13.6 us -> 0 us
  between operations: 13.3 us -> 0.01 us
  local copies, waits for them, and re-layouts: 5.87 us -> 1.47 us
    all_gather x2 -> x0, waiting for transfers between devices: 142 us -> none  [the longest x1 95.1 us: shards(): lax.all_gather(value_rows, 'seq', axis=0, tiled=True)]
    reduce_scatter x1 -> x0, waiting for transfers between devices: 126 us -> none  [shards(): lax.psum_scatter(partial_out, 'head', scatter_dimension=1, tiled=True)]
    pallas_call x0 -> x1, Pallas kernels: none -> 59.5 us  [shards(): pl.pallas_call(kernel, out_shape=jax.ShapeDtypeStruct((256, HD), bf16), i...]
    dot_general x33 -> x0, matrix products: 53.1 us -> none  [the longest x16 26.3 us: absorb_block(): jnp.einsum('rhk,kd->rhd', weights.astype(jnp.bfloat16), value_rows, prefe...]
    all_gather x1 -> x0, blocking collectives: 45 us -> none  [shards(): lax.all_gather(key_tags, 'seq', axis=0, tiled=True)]
    reduce_sum x17 -> x0, other arithmetic: 7.53 us -> none  [the longest x16 6.75 us: absorb_block(): totals = totals * correction + jnp.sum(weights, axis=-1)]
  transfers between devices with their start and end apart: 3 -> 0, of which waited for: 3 -> 0; matrix products, arithmetic and copies ran while one was open for 1% -> 0% of each run, Pallas kernels for 0% -> 0%
where the time goes in v1:
time: 61.4 us; the launch traced here: 61 us
  Pallas kernels  59.5 us (97%)
  local copies, waits for them, and re-layouts  1.47 us (2%)
    pallas_call x1, Pallas kernels, shards(): pl.pallas_call(kernel, out_shape=jax.ShapeDtypeStruct((256, HD), bf16), i...  59.5 us
    unnamed x1, local copies, waits for them, and re-layouts  1.47 us

profile of v1, /device:TPU:1, one launch (start us, length us, event | category | flops | bytes accessed | tf_op | source)
XLA Modules:
  0.0 61.0 jit_solution(17330757546869586026)
XLA Ops:
  0.0 59.5 %shard_map.91 = bf16[256,128]{1,0:T(8,128)(2,1)} custom-call(s32[8]{0:T(128)} %len_s.1, s32[256]{0:T(256)} %req_s.1, s32[2,128]{1,0:T(2,128)} %bitcast.2, s32[2,128]{1,0:T(2,128)} %bitcast.3, bf16[256,128]{1,0:T(8,128)(2,1)} %q_h.1, bf16[256,512]{1,0:T(8,128)(2,1)} %bk_h.1, bf16[256,512]{1,0:T(8,128)(2,1)} %bv_h.1, bf16[4,1024,128]{2,1,0:T(8,128)(2,1)} %ck_h.1, ...), custom_call_target="tpu_custom_call" | custom-call | tf_op jit(solution)/shard_map/pallas_call | solution.py:425
  59.5 1.5 %copy.11 = bf16[256,128]{1,0:T(8,128)(2,1)} copy(bf16[256,128]{1,0:T(8,128)(2,1)} %shard_map.91) | data formatting | bytes 131072

commit v2 on v1

--- a/solution.py
+++ b/solution.py
@@ -21,9 +21,9 @@
 
 
 def kernel(
-    len_s, req_s, req_v, pos_v, q_h, bk_h, bv_h, ck_h, cv_h, w_h,
+    len_h, req_h, rows_h, pos_h, q_h, bk_h, bv_h, ck_h, cv_h, w_h,
     out_ref,
-    qraw, kraw, cosb, sinb, qbuf, qhot, cand, gkv, bias, cks, cvs, qs, sp, spr,
+    len_s, req_s, req_v, pos_v, qraw, kraw, cosb, sinb, qbuf, qhot, cand, gkv, bias, cks, cvs, qs, sp, spr,
     ob, tb, lb, osend, ssend, orecv, srecv, hbuf, wbuf, psend, precv,
     loc, sq, rq, sc, rc, sz, rz, sg, rg, ss, rs, sw, rw, so, ro, sl, rl, sh, rh, sf, rf,
 ):
@@ -64,7 +64,11 @@
     c_cv = pltpu.make_async_copy(cv_h.at[g, pl.ds(mycand, 32)], cand.at[1, 0], loc.at[4])
     c_sk = pltpu.make_async_copy(ck_h.at[g], cks, loc.at[5])
     c_sv = pltpu.make_async_copy(cv_h.at[g], cvs, loc.at[6])
-    for c in (c_q, c_k, c_v, c_ck, c_cv, c_sk, c_sv):
+    c_small = [
+        pltpu.make_async_copy(src, dst, loc.at[8 + n])
+        for n, (src, dst) in enumerate(((rows_h, req_v), (pos_h, pos_v), (len_h, len_s), (req_h, req_s)))
+    ]
+    for c in c_small + [c_k, c_v, c_q, c_ck, c_cv, c_sk, c_sv]:
         c.start()
 
     barrier = pltpu.get_barrier_semaphore()
@@ -73,27 +77,6 @@
     peers += [fpeer(k) for k in (1, 3)]
     for peer in peers:
         pl.semaphore_signal(barrier, inc=1, device_id=peer, device_id_type=MESH)
-
-    row_len = jnp.zeros((2, 128), i32)
-    for r in range(REQS):
-        row_len = jnp.where(req_v[...] == r, len_s[r], row_len)
-    rotary = (row_len + pos_v[...]).astype(f32)
-    spread = jnp.concatenate(
-        [jnp.transpose(jnp.broadcast_to(rotary[h : h + 1, :], (128, 128))) for h in (0, 1)], axis=0
-    )
-    lane8 = lax.broadcasted_iota(i32, (8, 128), 1)
-    freqs = jnp.zeros((8, 128), f32)
-    for k in range(HD // 4):
-        freqs = jnp.where((lane8 < 64) & (lane8 % 32 == k), 10000.0 ** (-k / (HD // 4)), freqs)
-    angles = spread * freqs[0:1, :]
-    lane256 = lax.broadcasted_iota(i32, (256, 128), 1)
-    cosb[...] = jnp.cos(angles)
-    sine = jnp.sin(angles)
-    sinb[...] = jnp.where(lane256 < 32, -sine, sine)
-
-    def rotate(v, cosine, signed, lane):
-        partner = jnp.where(lane < 32, pltpu.roll(v, 96, 1), pltpu.roll(v, 32, 1))
-        return v * cosine + partner * signed
 
     pl.semaphore_wait(barrier, len(peers))
 
@@ -110,6 +93,55 @@
     for c in cand_c:
         c.start()
 
+    for c in c_small:
+        c.wait()
+    row_len = jnp.zeros((2, 128), i32)
+    for r in range(REQS):
+        row_len = jnp.where(req_v[...] == r, len_s[r], row_len)
+    rotary = (row_len + pos_v[...]).astype(f32)
+    spread = jnp.concatenate(
+        [jnp.transpose(jnp.broadcast_to(rotary[h : h + 1, :], (128, 128))) for h in (0, 1)], axis=0
+    )
+    lane8 = lax.broadcasted_iota(i32, (8, 128), 1)
+    turns = jnp.zeros((8, 128), f32)
+    for k in range(HD // 4):
+        turns = jnp.where(
+            (lane8 < 64) & (lane8 % 32 == k), 10000.0 ** (-k / (HD // 4)) / (2.0 * math.pi), turns
+        )
+    lane256 = lax.broadcasted_iota(i32, (256, 128), 1)
+    angle = spread * turns[0:1, :]
+    angle = (angle - jnp.floor(angle + 0.5)) * (2.0 * math.pi)
+    square = angle * angle
+    cosine = jnp.full((256, 128), 1.0 / math.factorial(16), f32)
+    sine = jnp.full((256, 128), -1.0 / math.factorial(15), f32)
+    for n in range(7, -1, -1):
+        cosine = cosine * square + (-1.0) ** n / math.factorial(2 * n)
+    for n in range(6, -1, -1):
+        sine = sine * square + (-1.0) ** n / math.factorial(2 * n + 1)
+    sine = sine * angle
+    cosb[...] = cosine
+    sinb[...] = jnp.where(lane256 < 32, -sine, sine)
+
+    def rotate(v, cosine, signed, lane):
+        partner = jnp.where(lane < 32, pltpu.roll(v, 96, 1), pltpu.roll(v, 32, 1))
+        return v * cosine + partner * signed
+
+    def spread_piece(kind, z):
+        src = gkv.at[kind, :, 0, 0, z]
+        for k in (3, 1, 2):
+            remote(src, gkv.at[kind, :, k, 0, z], sg.at[kind, k, 0], rg.at[kind, k, 0], gpeer(k, False)).start()
+        remote(src, gkv.at[kind, :, 0, 1, z], sg.at[kind, 0, 1], rg.at[kind, 0, 1], gpeer(0, True)).start()
+
+    def spread_all(kind):
+        cs = [
+            remote(gkv.at[kind, :, 0, 0], gkv.at[kind, :, k, 0], sg.at[kind, k, 0], rg.at[kind, k, 0], gpeer(k, False))
+            for k in (1, 2, 3)
+        ]
+        cs.append(
+            remote(gkv.at[kind, :, 0, 0], gkv.at[kind, :, 0, 1], sg.at[kind, 0, 1], rg.at[kind, 0, 1], gpeer(0, True))
+        )
+        return cs
+
     c_k.wait()
     gkv[0, 0, 0, 0, 0] = rotate(
         kraw[...].astype(f32), cosb[pl.ds(piece, 32), :], sinb[pl.ds(piece, 32), :],
@@ -118,6 +150,7 @@
     c_v.wait()
     for c in blk_c:
         c.start()
+    spread_piece(0, 0)
     c_q.wait()
     qbuf[0] = rotate(qraw[...].astype(f32), cosb[...], sinb[...], lane256).astype(bf16)
     for c in q_c:
@@ -133,9 +166,6 @@
                 pltpu.make_async_copy(src, dst, loc.at[7]).start()
             else:
                 remote(src, dst, sw.at[kc, ko], rw.at[kc, ko], gpeer(kc, ko == 1)).start()
-
-    blocks_start(0, 0)
-    blocks_start(0, 1)
 
     big = req_s[128]
     first = jnp.int32(0)
@@ -155,6 +185,22 @@
 
     def request_of(row):
         return jnp.where(row < big, row, jnp.where(row < big + BIG, big, row - (BIG - 1)))
+
+    key = lax.broadcasted_iota(i32, (1024, 128), 0)
+    lane1024 = lax.broadcasted_iota(i32, (1024, 128), 1)
+    key_chip = (chip + 4 - (key >> 8)) & 3
+    key_core = (core + (key >> 7)) & 1
+    key_z = (zh + 4 - (key >> 5)) & 3
+    inner = 32 * (key_chip * 2 + key_core) + (key & 31)
+    block_req = request_of(1024 * x + 256 * key_z + inner)
+    bias[0] = jnp.where(lane1024 == block_req, 0.0, MASKED).astype(bf16)
+    slot = 1024 * key_z + 256 * x + inner
+    inside = ((slot - first) & 4095) < span
+    bias[1] = jnp.where(inside & (lane1024 == big), 0.0, MASKED).astype(bf16)
+    row256 = lax.broadcasted_iota(i32, (256, 128), 0)
+    for k in range(4):
+        row = 256 * (4 * ((x + 4 - k) % 4) + zh) + row256
+        qhot[k] = jnp.where(lane256 == request_of(row), 1.0, 0.0).astype(bf16)
 
     for c in cand_c:
         c.wait_recv()
@@ -174,18 +220,43 @@
     ]
     for c in zc_c:
         c.start()
-
-    def spread_start(kind):
-        cs = [
-            remote(gkv.at[kind, :, 0, 0], gkv.at[kind, :, k, 0], sg.at[kind, k, 0], rg.at[kind, k, 0], gpeer(k, False))
-            for k in (1, 2, 3)
-        ]
-        cs.append(
-            remote(gkv.at[kind, :, 0, 0], gkv.at[kind, :, 0, 1], sg.at[kind, 0, 1], rg.at[kind, 0, 1], gpeer(0, True))
-        )
-        for c in cs:
-            c.start()
-        return cs
+    spread_piece(1, 0)
+
+    blk_c[1].wait_recv()
+    spread_piece(0, 1)
+    blk_c[2].wait_recv()
+    spread_piece(0, 3)
+
+    for c in q_c:
+        c.wait_recv()
+    at0, at3 = x, (x + 1) % 4
+    qs[0, 0:16, :] = qbuf[at0, 0:16, :]
+    qs[0, 16:32, :] = qbuf[at3, 240:256, :]
+    qs_c = [remote(qs.at[0], qs.at[k], ss.at[0, k], rs.at[0, k], zpeer(k)) for k in order]
+    for c in qs_c:
+        c.start()
+
+    row128 = lax.broadcasted_iota(i32, (128, 128), 0)
+    lane128 = lax.broadcasted_iota(i32, (128, 128), 1)
+    from_z = (zh + 4 - (row128 >> 5)) & 3
+    late = (row128 >> 4) & 1
+    qs_row = 256 * from_z + (row128 & 15) + late * (3072 + 240)
+    qs_hot = jnp.where(lane128 == request_of(qs_row), 1.0, 0.0).astype(bf16)
+    token = 1024 * seq + key
+    seen = (token >= low8[0:1, :]) & (token < high8[0:1, :])
+    bias[2] = jnp.where(seen, 0.0, MASKED).astype(bf16)
+    zc_c[1].wait_recv()
+    spread_piece(1, 1)
+    zc_c[2].wait_recv()
+    spread_piece(1, 3)
+    blk_c[0].wait_recv()
+    spread_piece(0, 2)
+    zc_c[0].wait_recv()
+    spread_piece(1, 2)
+    blk_g, cache_g = spread_all(0), spread_all(1)
+    blocks_start(0, 0)
+    blocks_start(0, 1)
+    blocks_start(1, 0)
 
     def relay(kind, cs):
         fs = []
@@ -203,39 +274,6 @@
         for f in fs:
             f.wait_recv()
 
-    for c in blk_c:
-        c.wait_recv()
-    blk_g = spread_start(0)
-
-    for c in q_c:
-        c.wait_recv()
-    at0, at3 = x, (x + 1) % 4
-    qs[0, 0:16, :] = qbuf[at0, 0:16, :]
-    qs[0, 16:32, :] = qbuf[at3, 240:256, :]
-    qs_c = [remote(qs.at[0], qs.at[k], ss.at[0, k], rs.at[0, k], zpeer(k)) for k in order]
-    for c in qs_c:
-        c.start()
-
-    for c in zc_c:
-        c.wait_recv()
-    cache_g = spread_start(1)
-
-    key = lax.broadcasted_iota(i32, (1024, 128), 0)
-    lane1024 = lax.broadcasted_iota(i32, (1024, 128), 1)
-    key_chip = (chip + 4 - (key >> 8)) & 3
-    key_core = (core + (key >> 7)) & 1
-    key_z = (zh + 4 - (key >> 5)) & 3
-    inner = 32 * (key_chip * 2 + key_core) + (key & 31)
-    block_req = request_of(1024 * x + 256 * key_z + inner)
-    bias[0] = jnp.where(lane1024 == block_req, 0.0, MASKED).astype(bf16)
-    slot = 1024 * key_z + 256 * x + inner
-    inside = ((slot - first) & 4095) < span
-    bias[1] = jnp.where(inside & (lane1024 == big), 0.0, MASKED).astype(bf16)
-    row256 = lax.broadcasted_iota(i32, (256, 128), 0)
-    for k in range(4):
-        row = 256 * (4 * ((x + 4 - k) % 4) + zh) + row256
-        qhot[k] = jnp.where(lane256 == request_of(row), 1.0, 0.0).astype(bf16)
-
     def attend(kind, k, v_t):
         k_aug = jnp.concatenate([gkv[kind, 0].reshape(1024, 128), bias[kind]], axis=1)
         q_aug = jnp.concatenate([qbuf[k], qhot[k]], axis=1)
@@ -255,18 +293,9 @@
         c.wait_recv()
     c_sk.wait()
     c_sv.wait()
-    row128 = lax.broadcasted_iota(i32, (128, 128), 0)
-    lane128 = lax.broadcasted_iota(i32, (128, 128), 1)
-    from_z = (zh + 4 - (row128 >> 5)) & 3
-    late = (row128 >> 4) & 1
-    qs_row = 256 * from_z + (row128 & 15) + late * (3072 + 240)
-    qs_hot = jnp.where(lane128 == request_of(qs_row), 1.0, 0.0).astype(bf16)
-    token = 1024 * seq + key
-    seen = (token >= low8[0:1, :]) & (token < high8[0:1, :])
-    own_bias = jnp.where(seen, 0.0, MASKED).astype(bf16)
     s = lax.dot_general(
         jnp.concatenate([qs[...].reshape(128, 128), qs_hot], axis=1),
-        jnp.concatenate([cks[...], own_bias], axis=1),
+        jnp.concatenate([cks[...], bias[2]], axis=1),
         (((1,), (1,)), ((), ())), preferred_element_type=f32,
     )
     top = jnp.max(s, axis=1, keepdims=True) * SCALE
@@ -297,9 +326,8 @@
     lax.fori_loop(0, 4, block_step, 0)
 
     cache_f = relay(1, cache_g)
-    for kc in (2, 1, 3):
-        blocks_start(kc, 0)
-        blocks_start(kc, 1)
+    for kc, ko in ((3, 0), (3, 1), (1, 1), (2, 0), (2, 1)):
+        blocks_start(kc, ko)
 
     for c in sp_c:
         c.wait_recv()
@@ -334,6 +362,8 @@
             o_c.append(remote(ssend.at[k], srecv.at[k], sl.at[k], rl.at[k], back))
             o_c[-2].start()
             o_c[-1].start()
+    for c in cand_c + q_c + blk_c + zc_c + blk_g + blk_f + cache_g + cache_f + qs_c + sp_c:
+        c.wait_send()
     for c in o_c:
         c.wait_recv()
 
@@ -400,6 +430,8 @@
         mids.append(mid)
         finals.append(near)
         own.append((acc[:, 0:128], acc[:, fwd * 128 : fwd * 128 + 128]))
+    for c in o_c + h_c[0] + h_c[1] + h_f[0] + h_f[1]:
+        c.wait_send()
     for half in (0, 1):
         fwd = 1 if half == 0 else 3
         mids[half].wait_recv()
@@ -407,14 +439,15 @@
         far = remote(psend.at[half, fwd], precv.at[half, fwd], sf.at[half, fwd], rf.at[half, fwd], fpeer(fwd))
         far.start()
         finals.append(far)
+    for c in w_wait:
+        c.wait_send()
     for half in (0, 1):
         finals[half].wait_recv()
         finals[2 + half].wait_recv()
         total = own[half][0] + precv[half, 1].astype(f32) + precv[half, 3].astype(f32)
         out_ref[128 * half : 128 * half + 128, :] = total.astype(bf16)
 
-    sent = cand_c + q_c + blk_c + zc_c + blk_g + blk_f + cache_g + cache_f + qs_c + sp_c
-    sent += w_wait + o_c + h_c[0] + h_c[1] + h_f[0] + h_f[1] + mids + finals
+    sent = mids + finals
     for c in sent:
         c.wait_send()
 
@@ -425,11 +458,13 @@
     return pl.pallas_call(
         kernel,
         out_shape=jax.ShapeDtypeStruct((256, HD), bf16),
-        in_specs=[pl.BlockSpec(memory_space=pltpu.SMEM)] * 2
-        + [pl.BlockSpec(memory_space=pltpu.VMEM)] * 2
-        + [pl.BlockSpec(memory_space=pl.ANY)] * 6,
+        in_specs=[pl.BlockSpec(memory_space=pl.ANY)] * 10,
         out_specs=pl.BlockSpec(memory_space=pltpu.VMEM),
         scratch_shapes=[
+            pltpu.SMEM((8,), i32),
+            pltpu.SMEM((256,), i32),
+            vmem((2, 128), i32),
+            vmem((2, 128), i32),
             vmem((256, 128), bf16),
             vmem((32, 128), bf16),
             vmem((256, 128), f32),
@@ -438,7 +473,7 @@
             vmem((4, 256, 128), bf16),
             vmem((2, 4, 32, 128), bf16),
             vmem((2, 2, 4, 2, 4, 32, 128), bf16),
-            vmem((2, 1024, 128), bf16),
+            vmem((3, 1024, 128), bf16),
             vmem((1024, 128), bf16),
             vmem((1024, 128), bf16),
             vmem((4, 32, 128), bf16),
@@ -455,7 +490,7 @@
             vmem((4, 2, 128, 512), bf16),
             vmem((2, 4, 128, 128), bf16),
             vmem((2, 4, 128, 128), bf16),
-            dma((8,)),
+            dma((12,)),
             dma((4,)), dma((4,)),
             dma((2, 4)), dma((2, 4)),
             dma((2, 4)), dma((2, 4)),

time: 61.4 us -> 61.4 us (level)
  the two profiles are of different devices: /device:TPU:1 before, /device:TPU:8 now
where the time goes in v2:
time: 61.4 us; the launch traced here: 61.3 us
  Pallas kernels  59.8 us (97%)
  local copies, waits for them, and re-layouts  1.47 us (2%)
    pallas_call x1, Pallas kernels, shards(): pl.pallas_call(kernel, out_shape=jax.ShapeDtypeStruct((256, HD), bf16), i...  59.8 us
    unnamed x1, local copies, waits for them, and re-layouts  1.47 us

profile of v2, /device:TPU:8, one launch (start us, length us, event | category | flops | bytes accessed | tf_op | source)
XLA Modules:
  0.0 61.3 jit_solution(9105679634508596639)
XLA Ops:
  0.0 59.8 %shard_map.91 = bf16[256,128]{1,0:T(8,128)(2,1)} custom-call(s32[8]{0:T(128)} %len_h.1, s32[256]{0:T(256)} %req_h.1, s32[2,128]{1,0:T(2,128)} %bitcast.2, s32[2,128]{1,0:T(2,128)} %bitcast.3, bf16[256,128]{1,0:T(8,128)(2,1)} %q_h.1, bf16[256,512]{1,0:T(8,128)(2,1)} %bk_h.1, bf16[256,512]{1,0:T(8,128)(2,1)} %bv_h.1, bf16[4,1024,128]{2,1,0:T(8,128)(2,1)} %ck_h.1, ...), custom_call_target="tpu_custom_call" | custom-call | tf_op jit(solution)/shard_map/pallas_call | solution.py:458
  59.8 1.5 %copy.11 = bf16[256,128]{1,0:T(8,128)(2,1)} copy(bf16[256,128]{1,0:T(8,128)(2,1)} %shard_map.91) | data formatting | bytes 131072

commit v3 on v2

--- a/solution.py
+++ b/solution.py
@@ -11,8 +11,7 @@
 REQS = 8
 BIG = 4089
 MASKED = -1e30
-SCALE = math.log2(math.e) / math.sqrt(HD)
-LN2 = math.log(2.0)
+SCALE = 1.0 / math.sqrt(HD)
 
 bf16 = jnp.bfloat16
 f32 = jnp.float32
@@ -22,10 +21,10 @@
 
 def kernel(
     len_h, req_h, rows_h, pos_h, q_h, bk_h, bv_h, ck_h, cv_h, w_h,
-    out_ref,
-    len_s, req_s, req_v, pos_v, qraw, kraw, cosb, sinb, qbuf, qhot, cand, gkv, bias, cks, cvs, qs, sp, spr,
-    ob, tb, lb, osend, ssend, orecv, srecv, hbuf, wbuf, psend, precv,
-    loc, sq, rq, sc, rc, sz, rz, sg, rg, ss, rs, sw, rw, so, ro, sl, rl, sh, rh, sf, rf,
+    mine_ref, near_ref,
+    len_s, req_s, req_v, pos_v, qraw, kraw, cosb, sinb, qbuf, qhot, cand, gkv, bias, cks, cvs, qx, qs, sp, spr,
+    ob, tb, lb, osend, ssend, orecv, srecv, hbuf, wfull, wst, wbuf, psend, precv, own, wts,
+    loc, sq, rq, sc, rc, sz, rz, sg, rg, ss, rs, sw, rw, sx, rx, so, ro, sl, rl, sh, rh, sf, rf,
 ):
     seq = lax.axis_index("seq")
     head = lax.axis_index("head")
@@ -68,7 +67,8 @@
         pltpu.make_async_copy(src, dst, loc.at[8 + n])
         for n, (src, dst) in enumerate(((rows_h, req_v), (pos_h, pos_v), (len_h, len_s), (req_h, req_s)))
     ]
-    for c in c_small + [c_k, c_v, c_q, c_ck, c_cv, c_sk, c_sv]:
+    c_w = pltpu.make_async_copy(w_h, wfull, loc.at[7])
+    for c in c_small + [c_k, c_v, c_q, c_ck, c_cv, c_sk, c_sv, c_w]:
         c.start()
 
     barrier = pltpu.get_barrier_semaphore()
@@ -153,19 +153,20 @@
     spread_piece(0, 0)
     c_q.wait()
     qbuf[0] = rotate(qraw[...].astype(f32), cosb[...], sinb[...], lane256).astype(bf16)
-    for c in q_c:
-        c.start()
-
-    def blocks_start(kc, ko):
+    qx[0, 0:16, :] = qbuf[0, 0:16, :]
+    qx[0, 16:32, :] = qbuf[0, 240:256, :]
+    qx_c = [remote(qx.at[0], qx.at[k], ss.at[2, k], rs.at[2, k], xpeer(k)) for k in order]
+    for c in qx_c + q_c:
+        c.start()
+
+    mine = x % 2
+
+    def block_copy(kc, ko):
         mm = ((chip + kc) % 4) * 2 + ((1 - core) if ko else core)
-        for j in range(4):
-            col = pl.multiple_of((((g + j) % 4) * 8 + mm) * 128, 128)
-            src = w_h.at[:, pl.ds(col, 128)]
-            dst = wbuf.at[kc, ko, :, j * 128 : (j + 1) * 128]
-            if kc == 0 and ko == 0:
-                pltpu.make_async_copy(src, dst, loc.at[7]).start()
-            else:
-                remote(src, dst, sw.at[kc, ko], rw.at[kc, ko], gpeer(kc, ko == 1)).start()
+        src, dst = wst.at[mm], wbuf.at[kc, ko]
+        if kc:
+            src, dst = src.at[mine], dst.at[mine]
+        return remote(src, dst, sw.at[kc, ko], rw.at[kc, ko], gpeer(kc, ko == 1))
 
     big = req_s[128]
     first = jnp.int32(0)
@@ -186,21 +187,38 @@
     def request_of(row):
         return jnp.where(row < big, row, jnp.where(row < big + BIG, big, row - (BIG - 1)))
 
-    key = lax.broadcasted_iota(i32, (1024, 128), 0)
-    lane1024 = lax.broadcasted_iota(i32, (1024, 128), 1)
-    key_chip = (chip + 4 - (key >> 8)) & 3
-    key_core = (core + (key >> 7)) & 1
-    key_z = (zh + 4 - (key >> 5)) & 3
-    inner = 32 * (key_chip * 2 + key_core) + (key & 31)
-    block_req = request_of(1024 * x + 256 * key_z + inner)
-    bias[0] = jnp.where(lane1024 == block_req, 0.0, MASKED).astype(bf16)
-    slot = 1024 * key_z + 256 * x + inner
-    inside = ((slot - first) & 4095) < span
-    bias[1] = jnp.where(inside & (lane1024 == big), 0.0, MASKED).astype(bf16)
+    c_w.wait()
+    for h in range(32):
+        for n in range(4):
+            wst[h % 8, n // 2, n % 2, (h // 8 + 4 - g) % 4] = wfull[n * 32 : n * 32 + 32, h * 128 : (h + 1) * 128]
+
+    row128 = lax.broadcasted_iota(i32, (128, 128), 0)
+    lane128 = lax.broadcasted_iota(i32, (128, 128), 1)
+    key_z = (zh + 4 - (row128 >> 5)) & 3
+
+    def mask_step(n, carry):
+        rows = pl.ds(pl.multiple_of(128 * n, 128), 128)
+        member = ((chip + 4 - n // 2) % 4) * 2 + (core + n) % 2
+        inner = 32 * member + (row128 & 31)
+        block_req = request_of(1024 * x + 256 * key_z + inner)
+        bias[0, rows, :] = jnp.where(lane128 == block_req, 0.0, MASKED).astype(bf16)
+        slot = 1024 * key_z + 256 * x + inner
+        inside = ((slot - first) & 4095) < span
+        bias[1, rows, :] = jnp.where(inside & (lane128 == big), 0.0, MASKED).astype(bf16)
+        token = 1024 * seq + 128 * n + row128
+        seen = (token >= low8[0:1, :]) & (token < high8[0:1, :])
+        bias[2, rows, :] = jnp.where(seen, 0.0, MASKED).astype(bf16)
+        return carry
+
+    lax.fori_loop(0, 8, mask_step, 0)
     row256 = lax.broadcasted_iota(i32, (256, 128), 0)
-    for k in range(4):
+
+    def hot_step(k, carry):
         row = 256 * (4 * ((x + 4 - k) % 4) + zh) + row256
         qhot[k] = jnp.where(lane256 == request_of(row), 1.0, 0.0).astype(bf16)
+        return carry
+
+    lax.fori_loop(0, 4, hot_step, 0)
 
     for c in cand_c:
         c.wait_recv()
@@ -222,29 +240,22 @@
         c.start()
     spread_piece(1, 0)
 
+    for c in qx_c:
+        c.wait_recv()
+    at0, at3 = x, (x + 1) % 4
+    qs[0, 0:16, :] = qx[at0, 0:16, :]
+    qs[0, 16:32, :] = qx[at3, 16:32, :]
+    qs_c = [remote(qs.at[0], qs.at[k], ss.at[0, k], rs.at[0, k], zpeer(k)) for k in order]
+    for c in qs_c:
+        c.start()
     blk_c[1].wait_recv()
     spread_piece(0, 1)
     blk_c[2].wait_recv()
     spread_piece(0, 3)
 
-    for c in q_c:
-        c.wait_recv()
-    at0, at3 = x, (x + 1) % 4
-    qs[0, 0:16, :] = qbuf[at0, 0:16, :]
-    qs[0, 16:32, :] = qbuf[at3, 240:256, :]
-    qs_c = [remote(qs.at[0], qs.at[k], ss.at[0, k], rs.at[0, k], zpeer(k)) for k in order]
-    for c in qs_c:
-        c.start()
-
-    row128 = lax.broadcasted_iota(i32, (128, 128), 0)
-    lane128 = lax.broadcasted_iota(i32, (128, 128), 1)
-    from_z = (zh + 4 - (row128 >> 5)) & 3
     late = (row128 >> 4) & 1
-    qs_row = 256 * from_z + (row128 & 15) + late * (3072 + 240)
+    qs_row = 256 * key_z + (row128 & 15) + late * (3072 + 240)
     qs_hot = jnp.where(lane128 == request_of(qs_row), 1.0, 0.0).astype(bf16)
-    token = 1024 * seq + key
-    seen = (token >= low8[0:1, :]) & (token < high8[0:1, :])
-    bias[2] = jnp.where(seen, 0.0, MASKED).astype(bf16)
     zc_c[1].wait_recv()
     spread_piece(1, 1)
     zc_c[2].wait_recv()
@@ -254,9 +265,9 @@
     zc_c[0].wait_recv()
     spread_piece(1, 2)
     blk_g, cache_g = spread_all(0), spread_all(1)
-    blocks_start(0, 0)
-    blocks_start(0, 1)
-    blocks_start(1, 0)
+    w_c = [block_copy(kc, ko) for kc, ko in ((0, 1), (1, 0), (3, 0), (3, 1), (1, 1), (2, 0), (2, 1))]
+    for c in w_c:
+        c.start()
 
     def relay(kind, cs):
         fs = []
@@ -279,14 +290,17 @@
         q_aug = jnp.concatenate([qbuf[k], qhot[k]], axis=1)
         s = lax.dot_general(k_aug, q_aug, (((1,), (1,)), ((), ())), preferred_element_type=f32)
         top = jnp.max(s, axis=0, keepdims=True) * SCALE
-        p = jnp.exp2(s * SCALE - top)
-        total = jnp.sum(p, axis=0, keepdims=True)
+        p = jnp.exp(s * SCALE - top)
         o = jnp.dot(v_t, p.astype(bf16), preferred_element_type=f32)
-        return o, top, total
+        return o[0:128, :], top, o[128:129, :]
+
+    def values(kind):
+        v = jnp.transpose(gkv[kind, 1].reshape(1024, 128))
+        return jnp.concatenate([v, jnp.ones((16, 1024), bf16)], axis=0)
 
     def merge(o1, t1, l1, o2, t2, l2):
         top = jnp.maximum(t1, t2)
-        w1, w2 = jnp.exp2(t1 - top), jnp.exp2(t2 - top)
+        w1, w2 = jnp.exp(t1 - top), jnp.exp(t2 - top)
         return o1 * w1 + o2 * w2, top, l1 * w1 + l2 * w2
 
     for c in qs_c:
@@ -299,10 +313,10 @@
         (((1,), (1,)), ((), ())), preferred_element_type=f32,
     )
     top = jnp.max(s, axis=1, keepdims=True) * SCALE
-    p = jnp.exp2(s * SCALE - top)
+    p = jnp.exp(s * SCALE - top)
     total = jnp.sum(p, axis=1, keepdims=True)
     o = jnp.dot(p.astype(bf16), cvs[...], preferred_element_type=f32) / total
-    lse = jnp.broadcast_to(top + jnp.log(total) * (1.0 / LN2), (128, 128))
+    lse = jnp.broadcast_to(top + jnp.log(total), (128, 128))
     sp[:, 0] = o.reshape(4, 32, 128)
     sp[:, 1] = lse.reshape(4, 32, 128)
     sp_c = [
@@ -312,9 +326,11 @@
         c.start()
 
     blk_f = relay(0, blk_g)
+    for c in q_c:
+        c.wait_recv()
     relay_wait(blk_g, blk_f)
 
-    vt0 = jnp.transpose(gkv[0, 1].reshape(1024, 128))
+    vt0 = values(0)
 
     def block_step(k, carry):
         o, t, l = attend(0, k, vt0)
@@ -326,8 +342,6 @@
     lax.fori_loop(0, 4, block_step, 0)
 
     cache_f = relay(1, cache_g)
-    for kc, ko in ((3, 0), (3, 1), (1, 1), (2, 0), (2, 1)):
-        blocks_start(kc, ko)
 
     for c in sp_c:
         c.wait_recv()
@@ -336,48 +350,66 @@
         o, t, l = merge(o, t, l, spr[k, 0], spr[k, 1], 1.0)
     pad = jnp.zeros((96, 128), f32)
     o, t, l = [jnp.transpose(jnp.concatenate([a, pad], axis=0)) for a in (o, t, l)]
-    for at, half, shift, own in ((at0, 0, 0, lane128 < 16), (at3, 1, 96, lane128 >= 112)):
+    for at, half, shift, put in ((at0, 0, 0, lane128 < 16), (at3, 1, 96, lane128 >= 112)):
         cols = slice(128 * half, 128 * half + 128)
         o2, t2, l2 = [pltpu.roll(a, shift, 1) if shift else a for a in (o, t, l)]
-        t2 = jnp.where(own, t2, MASKED)[0:8, :]
+        t2 = jnp.where(put, t2, MASKED)[0:8, :]
         l2 = l2[0:8, :]
         t1, l1 = tb[at, :, cols], lb[at, :, cols]
         top = jnp.maximum(t1, t2)
-        w1, w2 = jnp.exp2(t1 - top), jnp.exp2(t2 - top)
+        w1, w2 = jnp.exp(t1 - top), jnp.exp(t2 - top)
         tb[at, :, cols] = top
         lb[at, :, cols] = l1 * w1 + l2 * w2
-        ob[at, :, cols] = ob[at, :, cols] * w1[0:1, :] + jnp.where(own, o2, 0.0) * w2[0:1, :]
+        ob[at, :, cols] = ob[at, :, cols] * w1[0:1, :] + jnp.where(put, o2, 0.0) * w2[0:1, :]
 
     relay_wait(cache_g, cache_f)
-    vt1 = jnp.transpose(gkv[1, 1].reshape(1024, 128))
-    o_c = []
-    for k in order + (0,):
+    vt1 = values(1)
+
+    def back(k):
+        return (((x + 4 - k) % 4) * 4 + zh, head)
+
+    def o_copy(k):
+        return remote(osend.at[k], orecv.at[k], so.at[k], ro.at[k], back(k))
+
+    def l_copy(k):
+        return remote(ssend.at[k], srecv.at[k], sl.at[k], rl.at[k], back(k))
+
+    def cache_step(n, carry):
+        k = (2 + 3 * n + 3 * (n // 2) + 2 * (n // 3)) % 4
         o, t, l = attend(1, k, vt1)
         o, t, l = merge(ob[k], tb[k, 0:1, :], lb[k, 0:1, :], o, t, l)
         osend[k] = (o * (1.0 / l)).astype(bf16)
-        ssend[k] = jnp.broadcast_to(t + jnp.log(l) * (1.0 / LN2), (8, 256))
-        if k:
-            back = (((x + 4 - k) % 4) * 4 + zh, head)
-            o_c.append(remote(osend.at[k], orecv.at[k], so.at[k], ro.at[k], back))
-            o_c.append(remote(ssend.at[k], srecv.at[k], sl.at[k], rl.at[k], back))
-            o_c[-2].start()
-            o_c[-1].start()
-    for c in cand_c + q_c + blk_c + zc_c + blk_g + blk_f + cache_g + cache_f + qs_c + sp_c:
+        ssend[k] = jnp.broadcast_to(t + jnp.log(l), (8, 256))
+
+        @pl.when(n < 3)
+        def _():
+            o_copy(k).start()
+            l_copy(k).start()
+
+        return carry
+
+    lax.fori_loop(0, 4, cache_step, 0)
+    o_c = [f(k) for k in order for f in (o_copy, l_copy)]
+
+    for c in w_c[1:]:
+        c.wait_recv()
+    w_x = [
+        remote(wbuf.at[1:4, :, mine, n], wbuf.at[1:4, :, mine, n], sx.at[n], rx.at[n], xpeer(k))
+        for n, k in ((0, 3), (1, 1))
+    ]
+    for c in w_x:
+        c.start()
+    for c in cand_c + q_c + blk_c + zc_c + blk_g + blk_f + cache_g + cache_f + qx_c + qs_c + sp_c:
         c.wait_send()
     for c in o_c:
         c.wait_recv()
 
     lses = [ssend[0, 0:1, :]] + [srecv[k, 0:1, :] for k in (1, 2, 3)]
     top = jnp.maximum(jnp.maximum(lses[0], lses[1]), jnp.maximum(lses[2], lses[3]))
-    weights = [jnp.exp2(l - top) for l in lses]
+    weights = [jnp.exp(l - top) for l in lses]
     total = 1.0 / (weights[0] + weights[1] + weights[2] + weights[3])
-    h_c = []
-    for half in (0, 1):
-        cols = slice(128 * half, 128 * half + 128)
-        heads = osend[0, :, cols].astype(f32) * (weights[0] * total)[:, cols]
-        for k in (1, 2, 3):
-            heads = heads + orecv[k, :, cols].astype(f32) * (weights[k] * total)[:, cols]
-        hbuf[half, 0, 0] = jnp.transpose(heads).astype(bf16)
+
+    def h_copies(half):
         cs = [
             remote(
                 hbuf.at[half, 0, 0], hbuf.at[half, k, 0], sh.at[half, k, 0], rh.at[half, k, 0], gpeer(k, False)
@@ -387,9 +419,23 @@
         cs.append(
             remote(hbuf.at[half, 0, 0], hbuf.at[half, 0, 1], sh.at[half, 0, 1], rh.at[half, 0, 1], gpeer(0, True))
         )
-        for c in cs:
+        return cs
+
+    for k in range(4):
+        wts[k] = jnp.broadcast_to(weights[k] * total, (8, 256))
+
+    def heads_step(half, carry):
+        cols = pl.ds(pl.multiple_of(128 * half, 128), 128)
+        heads = osend[0, :, cols].astype(f32) * wts[0, 0:1, cols]
+        for k in (1, 2, 3):
+            heads = heads + orecv[k, :, cols].astype(f32) * wts[k, 0:1, cols]
+        hbuf[half, 0, 0] = jnp.transpose(heads).astype(bf16)
+        for c in h_copies(half):
             c.start()
-        h_c.append(cs)
+        return carry
+
+    lax.fori_loop(0, 2, heads_step, 0)
+    h_c = [h_copies(0), h_copies(1)]
     h_f = []
     for half in (0, 1):
         fs = []
@@ -402,50 +448,57 @@
             fs.append(f)
         h_f.append(fs)
 
-    w_wait = []
-    for kc in range(4):
-        for ko in (0, 1):
-            if kc or ko:
-                w_wait.append(
-                    remote(w_h.at[:, 0:512], wbuf.at[kc, ko], sw.at[kc, ko], rw.at[kc, ko], gpeer(kc, ko == 1))
-                )
-    for c in w_wait:
-        c.wait_recv()
-    pltpu.make_async_copy(w_h.at[:, 0:512], wbuf.at[0, 0], loc.at[7]).wait()
-
-    own, mids, finals = [], [], []
-    for half in (0, 1):
-        h_c[half][3].wait_recv()
-        for f in h_f[half]:
-            f.wait_recv()
+    for c in w_c[:1] + w_x:
+        c.wait_recv()
+    wbuf[0, 0] = wst[m]
+
+    def mid_copy(half):
+        return remote(psend.at[half, 2], precv.at[half], sf.at[half, 0], rf.at[half, 0], fpeer(1 + 2 * half))
+
+    def final_copy(half, j):
+        rows = pl.ds(pl.multiple_of(128 * half, 128), 128)
+        return remote(psend.at[half, j], near_ref.at[j // 2, rows], sf.at[half, j], rf.at[half, j], fpeer(j))
+
+    def mine_copy(half):
+        rows = pl.ds(pl.multiple_of(128 * half, 128), 128)
+        return pltpu.make_async_copy(own.at[half, 0], mine_ref.at[rows], loc.at[half])
+
+    def project_step(half, carry):
+        for c in h_copies(half)[3:]:
+            c.wait_recv()
+        for k in order:
+            remote(
+                hbuf.at[half, k, 0], hbuf.at[half, k, 1], sh.at[half, k, 1], rh.at[half, k, 1], gpeer(0, True)
+            ).wait_recv()
         lhs = jnp.concatenate([hbuf[half, kc, ko] for kc in range(4) for ko in (0, 1)], axis=1)
-        acc = jnp.dot(lhs, wbuf[...].reshape(1024, 512), preferred_element_type=f32)
-        fwd, bwd = (1, 3) if half == 0 else (3, 1)
-        psend[half, 2] = acc[:, 256:384].astype(bf16)
-        psend[half, bwd] = acc[:, bwd * 128 : bwd * 128 + 128].astype(bf16)
-        mid = remote(psend.at[half, 2], precv.at[half, 2], sf.at[half, 2], rf.at[half, 2], fpeer(fwd))
-        near = remote(psend.at[half, bwd], precv.at[half, bwd], sf.at[half, bwd], rf.at[half, bwd], fpeer(bwd))
-        mid.start()
-        near.start()
-        mids.append(mid)
-        finals.append(near)
-        own.append((acc[:, 0:128], acc[:, fwd * 128 : fwd * 128 + 128]))
+        rhs = jnp.concatenate([wbuf[:, :, :, :, j].reshape(1024, 128) for j in range(4)], axis=1)
+        acc = jnp.dot(lhs, rhs, preferred_element_type=f32)
+        for j in range(4):
+            own[half, j] = acc[:, j * 128 : (j + 1) * 128]
+            psend[half, j] = own[half, j].astype(bf16)
+        mid_copy(half).start()
+        final_copy(half, 3 - 2 * half).start()
+        mine_copy(half).start()
+        return carry
+
+    lax.fori_loop(0, 2, project_step, 0)
+    mids = [mid_copy(0), mid_copy(1)]
+    finals = [final_copy(0, 3), final_copy(1, 1)]
     for c in o_c + h_c[0] + h_c[1] + h_f[0] + h_f[1]:
         c.wait_send()
     for half in (0, 1):
         fwd = 1 if half == 0 else 3
         mids[half].wait_recv()
-        psend[half, fwd] = (own[half][1] + precv[half, 2].astype(f32)).astype(bf16)
-        far = remote(psend.at[half, fwd], precv.at[half, fwd], sf.at[half, fwd], rf.at[half, fwd], fpeer(fwd))
+        psend[half, fwd] = (own[half, fwd] + precv[half].astype(f32)).astype(bf16)
+        far = final_copy(half, fwd)
         far.start()
         finals.append(far)
-    for c in w_wait:
+    for c in w_c + w_x:
         c.wait_send()
     for half in (0, 1):
         finals[half].wait_recv()
         finals[2 + half].wait_recv()
-        total = own[half][0] + precv[half, 1].astype(f32) + precv[half, 3].astype(f32)
-        out_ref[128 * half : 128 * half + 128, :] = total.astype(bf16)
+        mine_copy(half).wait()
 
     sent = mids + finals
     for c in sent:
@@ -455,11 +508,11 @@
 def shards(queries, block_keys, block_values, cache_keys, cache_values, lengths, row_request, positions, out_weight):
     dma = pltpu.SemaphoreType.DMA
     vmem = pltpu.VMEM
-    return pl.pallas_call(
+    mine, near = pl.pallas_call(
         kernel,
-        out_shape=jax.ShapeDtypeStruct((256, HD), bf16),
+        out_shape=(jax.ShapeDtypeStruct((256, HD), f32), jax.ShapeDtypeStruct((2, 256, HD), bf16)),
         in_specs=[pl.BlockSpec(memory_space=pl.ANY)] * 10,
-        out_specs=pl.BlockSpec(memory_space=pltpu.VMEM),
+        out_specs=(pl.BlockSpec(memory_space=pl.ANY), pl.BlockSpec(memory_space=pl.ANY)),
         scratch_shapes=[
             pltpu.SMEM((8,), i32),
             pltpu.SMEM((256,), i32),
@@ -477,6 +530,7 @@
             vmem((1024, 128), bf16),
             vmem((1024, 128), bf16),
             vmem((4, 32, 128), bf16),
+            vmem((4, 32, 128), bf16),
             vmem((4, 2, 32, 128), f32),
             vmem((4, 2, 32, 128), f32),
             vmem((4, 128, 256), f32),
@@ -487,16 +541,21 @@
             vmem((4, 128, 256), bf16),
             vmem((4, 8, 256), f32),
             vmem((2, 4, 2, 128, 128), bf16),
-            vmem((4, 2, 128, 512), bf16),
+            vmem((128, 4096), bf16),
+            vmem((8, 2, 2, 4, 32, 128), bf16),
+            vmem((4, 2, 2, 2, 4, 32, 128), bf16),
             vmem((2, 4, 128, 128), bf16),
-            vmem((2, 4, 128, 128), bf16),
+            vmem((2, 128, 128), bf16),
+            vmem((2, 4, 128, 128), f32),
+            vmem((4, 8, 256), f32),
             dma((12,)),
             dma((4,)), dma((4,)),
             dma((2, 4)), dma((2, 4)),
             dma((2, 4)), dma((2, 4)),
             dma((2, 4, 2)), dma((2, 4, 2)),
-            dma((2, 4)), dma((2, 4)),
+            dma((3, 4)), dma((3, 4)),
             dma((4, 2)), dma((4, 2)),
+            dma((2,)), dma((2,)),
             dma((4,)), dma((4,)),
             dma((4,)), dma((4,)),
             dma((2, 4, 2)), dma((2, 4, 2)),
@@ -509,6 +568,7 @@
         lengths, row_request, row_request.reshape(2, 128), positions.reshape(2, 128),
         queries, block_keys, block_values, cache_keys, cache_values, out_weight,
     )
+    return (mine + near[0].astype(f32) + near[1].astype(f32)).astype(bf16)
 
 
 def solution(mesh):

time: 61.4 us -> 60.8 us (level)
  the two profiles are of different devices: /device:TPU:8 before, /device:TPU:1 now
where the time goes in v3:
time: 60.8 us; the launch traced here: 60.7 us
  Pallas kernels  59.1 us (97%)
  other arithmetic  1.6 us (3%)
    pallas_call x1, Pallas kernels, shards(): pl.pallas_call(kernel, out_shape=(jax.ShapeDtypeStruct((256, HD), f32), j...  59.1 us
    convert_element_type x1, other arithmetic, shards(): return (mine + near[0].astype(f32) + near[1].astype(f32)).astype(bf16)  1.6 us

profile of v3, /device:TPU:1, one launch (start us, length us, event | category | flops | bytes accessed | tf_op | source)
XLA Modules:
  0.0 60.7 jit_solution(3624052440515737405)
XLA Ops:
  0.0 59.1 %shard_map.91 = (f32[256,128]{1,0:T(8,128)}, bf16[2,256,128]{2,1,0:T(8,128)(2,1)}) custom-call(s32[8]{0:T(128)} %len_h.1, s32[256]{0:T(256)} %req_h.1, s32[2,128]{1,0:T(2,128)} %bitcast.8, s32[2,128]{1,0:T(2,128)} %bitcast.9, bf16[256,128]{1,0:T(8,128)(2,1)} %q_h.1, bf16[256,512]{1,0:T(8,128)(2,1)} %bk_h.1, bf16[256,512]{1,0:T(8,128)(2,1)} %bv_h.1, ...), custom_call_target="tpu_custom_call" | custom-call | tf_op jit(solution)/shard_map/pallas_call | solution.py:511
  59.1 1.6 %fusion = bf16[256,128]{1,0:T(8,128)(2,1)} fusion(f32[256,128]{1,0:T(8,128)} %get-tuple-element.7, bf16[2,256,128]{2,1,0:T(8,128)(2,1)} %get-tuple-element.8), kind=kLoop, calls=%fused_computation.1 | loop fusion | flops 163840 | bytes 327680 | tf_op jit(solution)/shard_map/convert_element_type | solution.py:571

commit v4 on v3

--- a/solution.py
+++ b/solution.py
@@ -24,7 +24,7 @@
     mine_ref, near_ref,
     len_s, req_s, req_v, pos_v, qraw, kraw, cosb, sinb, qbuf, qhot, cand, gkv, bias, cks, cvs, qx, qs, sp, spr,
     ob, tb, lb, osend, ssend, orecv, srecv, hbuf, wfull, wst, wbuf, psend, precv, own, wts,
-    loc, sq, rq, sc, rc, sz, rz, sg, rg, ss, rs, sw, rw, sx, rx, so, ro, sl, rl, sh, rh, sf, rf,
+    loc, sq, rq, sc, rc, sz, rz, sg, rg, sd, rd, ss, rs, sw, rw, sx, rx, so, ro, sl, rl, sh, rh, sf, rf,
 ):
     seq = lax.axis_index("seq")
     head = lax.axis_index("head")
@@ -81,13 +81,14 @@
     pl.semaphore_wait(barrier, len(peers))
 
     order = (2, 1, 3)
+    place = (0, 1, 3, 2)
     cand_c, q_c, blk_c = [], [], []
     for k in order:
         start = pl.multiple_of(256 * ((x + k) % 4) + 32 * m, 32)
         cand_c.append(remote(ck_h.at[g, pl.ds(start, 32)], cand.at[0, k], sc.at[0, k], rc.at[0, k], xpeer(k)))
         cand_c.append(remote(cv_h.at[g, pl.ds(start, 32)], cand.at[1, k], sc.at[1, k], rc.at[1, k], xpeer(k)))
         blk_c.append(
-            remote(gkv.at[0, :, 0, 0, 0], gkv.at[0, :, 0, 0, k], sz.at[0, k], rz.at[0, k], zpeer(k))
+            remote(gkv.at[0, :, 0, 0, 0], gkv.at[0, :, 0, 0, place[k]], sz.at[0, k], rz.at[0, k], zpeer(k))
         )
         q_c.append(remote(qbuf.at[0], qbuf.at[k], sq.at[k], rq.at[k], xpeer(k)))
     for c in cand_c:
@@ -127,19 +128,29 @@
         return v * cosine + partner * signed
 
     def spread_piece(kind, z):
-        src = gkv.at[kind, :, 0, 0, z]
+        src = gkv.at[kind, :, 0, 0, place[z]]
         for k in (3, 1, 2):
-            remote(src, gkv.at[kind, :, k, 0, z], sg.at[kind, k, 0], rg.at[kind, k, 0], gpeer(k, False)).start()
-        remote(src, gkv.at[kind, :, 0, 1, z], sg.at[kind, 0, 1], rg.at[kind, 0, 1], gpeer(0, True)).start()
+            remote(
+                src, gkv.at[kind, :, k, 0, place[z]], sg.at[kind, k, 0], rg.at[kind, k, 0], gpeer(k, False)
+            ).start()
+        remote(
+            src, gkv.at[kind, :, 0, 1, place[z]], sg.at[kind, 0, 1], rg.at[kind, 0, 1], gpeer(0, True)
+        ).start()
+
+    def far_copies():
+        return [
+            remote(gkv.at[1, :, 0, 0, 3], gkv.at[1, :, k, o, 3], sd.at[k, o], rd.at[k, o], gpeer(k, o == 1))
+            for k in (3, 1, 2, 0) for o in (0, 1) if k or o
+        ]
 
     def spread_all(kind):
+        upto = slice(0, 4 - kind)
+        src = gkv.at[kind, :, 0, 0, upto]
         cs = [
-            remote(gkv.at[kind, :, 0, 0], gkv.at[kind, :, k, 0], sg.at[kind, k, 0], rg.at[kind, k, 0], gpeer(k, False))
+            remote(src, gkv.at[kind, :, k, 0, upto], sg.at[kind, k, 0], rg.at[kind, k, 0], gpeer(k, False))
             for k in (1, 2, 3)
         ]
-        cs.append(
-            remote(gkv.at[kind, :, 0, 0], gkv.at[kind, :, 0, 1], sg.at[kind, 0, 1], rg.at[kind, 0, 1], gpeer(0, True))
-        )
+        cs.append(remote(src, gkv.at[kind, :, 0, 1, upto], sg.at[kind, 0, 1], rg.at[kind, 0, 1], gpeer(0, True)))
         return cs
 
     c_k.wait()
@@ -194,7 +205,9 @@
 
     row128 = lax.broadcasted_iota(i32, (128, 128), 0)
     lane128 = lax.broadcasted_iota(i32, (128, 128), 1)
-    key_z = (zh + 4 - (row128 >> 5)) & 3
+    from_z = (zh + 4 - (row128 >> 5)) & 3
+    lies = (row128 >> 5) & 3
+    key_z = (zh + 4 - (lies ^ (lies >> 1))) & 3
 
     def mask_step(n, carry):
         rows = pl.ds(pl.multiple_of(128 * n, 128), 128)
@@ -233,7 +246,7 @@
             chosen = jnp.where(ok, cand[t, k].astype(f32), chosen)
         gkv[1, t, 0, 0, 0] = chosen.astype(bf16)
     zc_c = [
-        remote(gkv.at[1, :, 0, 0, 0], gkv.at[1, :, 0, 0, k], sz.at[1, k], rz.at[1, k], zpeer(k))
+        remote(gkv.at[1, :, 0, 0, 0], gkv.at[1, :, 0, 0, place[k]], sz.at[1, k], rz.at[1, k], zpeer(k))
         for k in order
     ]
     for c in zc_c:
@@ -254,7 +267,7 @@
     spread_piece(0, 3)
 
     late = (row128 >> 4) & 1
-    qs_row = 256 * key_z + (row128 & 15) + late * (3072 + 240)
+    qs_row = 256 * from_z + (row128 & 15) + late * (3072 + 240)
     qs_hot = jnp.where(lane128 == request_of(qs_row), 1.0, 0.0).astype(bf16)
     zc_c[1].wait_recv()
     spread_piece(1, 1)
@@ -263,18 +276,22 @@
     blk_c[0].wait_recv()
     spread_piece(0, 2)
     zc_c[0].wait_recv()
-    spread_piece(1, 2)
+    far_c = far_copies()
+    for c in far_c:
+        c.start()
     blk_g, cache_g = spread_all(0), spread_all(1)
     w_c = [block_copy(kc, ko) for kc, ko in ((0, 1), (1, 0), (3, 0), (3, 1), (1, 1), (2, 0), (2, 1))]
     for c in w_c:
         c.start()
 
     def relay(kind, cs):
+        upto = slice(0, 4 - kind)
         fs = []
         for k in (1, 2, 3):
             cs[k - 1].wait_recv()
             f = remote(
-                gkv.at[kind, :, k, 0], gkv.at[kind, :, k, 1], sg.at[kind, k, 1], rg.at[kind, k, 1], gpeer(0, True)
+                gkv.at[kind, :, k, 0, upto], gkv.at[kind, :, k, 1, upto], sg.at[kind, k, 1], rg.at[kind, k, 1],
+                gpeer(0, True),
             )
             f.start()
             fs.append(f)
@@ -328,6 +345,7 @@
     blk_f = relay(0, blk_g)
     for c in q_c:
         c.wait_recv()
+    cache_f = relay(1, cache_g)
     relay_wait(blk_g, blk_f)
 
     vt0 = values(0)
@@ -341,7 +359,6 @@
 
     lax.fori_loop(0, 4, block_step, 0)
 
-    cache_f = relay(1, cache_g)
 
     for c in sp_c:
         c.wait_recv()
@@ -363,6 +380,8 @@
         ob[at, :, cols] = ob[at, :, cols] * w1[0:1, :] + jnp.where(put, o2, 0.0) * w2[0:1, :]
 
     relay_wait(cache_g, cache_f)
+    for c in far_c:
+        c.wait_recv()
     vt1 = values(1)
 
     def back(k):
@@ -399,7 +418,7 @@
     ]
     for c in w_x:
         c.start()
-    for c in cand_c + q_c + blk_c + zc_c + blk_g + blk_f + cache_g + cache_f + qx_c + qs_c + sp_c:
+    for c in cand_c + q_c + blk_c + zc_c + blk_g + blk_f + cache_g + cache_f + far_c + qx_c + qs_c + sp_c:
         c.wait_send()
     for c in o_c:
         c.wait_recv()
@@ -553,6 +572,7 @@
             dma((2, 4)), dma((2, 4)),
             dma((2, 4)), dma((2, 4)),
             dma((2, 4, 2)), dma((2, 4, 2)),
+            dma((4, 2)), dma((4, 2)),
             dma((3, 4)), dma((3, 4)),
             dma((4, 2)), dma((4, 2)),
             dma((2,)), dma((2,)),

time: 60.8 us -> 61.7 us (1.015)
  no operation moved by 1% of the time
where the time goes in v4:
time: 61.7 us; the launch traced here: 61.2 us
  Pallas kernels  59.6 us (97%)
  other arithmetic  1.6 us (3%)
    pallas_call x1, Pallas kernels, shards(): pl.pallas_call(kernel, out_shape=(jax.ShapeDtypeStruct((256, HD), f32), j...  59.6 us
    convert_element_type x1, other arithmetic, shards(): return (mine + near[0].astype(f32) + near[1].astype(f32)).astype(bf16)  1.6 us

profile of v4, /device:TPU:1, one launch (start us, length us, event | category | flops | bytes accessed | tf_op | source)
XLA Modules:
  0.0 61.2 jit_solution(11229708964246476373)
XLA Ops:
  0.0 59.6 %shard_map.91 = (f32[256,128]{1,0:T(8,128)}, bf16[2,256,128]{2,1,0:T(8,128)(2,1)}) custom-call(s32[8]{0:T(128)} %len_h.1, s32[256]{0:T(256)} %req_h.1, s32[2,128]{1,0:T(2,128)} %bitcast.8, s32[2,128]{1,0:T(2,128)} %bitcast.9, bf16[256,128]{1,0:T(8,128)(2,1)} %q_h.1, bf16[256,512]{1,0:T(8,128)(2,1)} %bk_h.1, bf16[256,512]{1,0:T(8,128)(2,1)} %bv_h.1, ...), custom_call_target="tpu_custom_call" | custom-call | tf_op jit(solution)/shard_map/pallas_call | solution.py:530
  59.6 1.6 %fusion = bf16[256,128]{1,0:T(8,128)(2,1)} fusion(f32[256,128]{1,0:T(8,128)} %get-tuple-element.7, bf16[2,256,128]{2,1,0:T(8,128)(2,1)} %get-tuple-element.8), kind=kLoop, calls=%fused_computation.1 | loop fusion | flops 163840 | bytes 327680 | tf_op jit(solution)/shard_map/convert_element_type | solution.py:591
